TPU v7x, 32 devices: a whole 2x2x4 slice. The times are simulated.
32 devices in a mesh: leaf: 8 (over z, x), group: 4 (over y, core).
Axes of the slice: x: 2, y: 2, z: 4, core: 2. Of those that a mesh axis runs over, the one named last changes fastest.
Arguments:
- q_two: float32 [65536, 256], P(('group', 'leaf'))
- q_one: float32 [65536, 256], P(('group', 'leaf'))
- sources: float32 [65536, 256], P(('group', 'leaf'))
- coupling_two: float32 [2, 256, 256], replicated, as said below
- coupling_one: float32 [256, 256], replicated, as said below
Outputs:
- panel_one: float32 [65536, 256], P(('group', 'leaf'))
- solution: float32 [65536, 256], P(('group', 'leaf'))
Inputs may be any that keep to these rules, and one draw needn't show every extreme that they name: coupling_two[0], coupling_two[1] and coupling_one are symmetric and positive definite. `coupling_one`: symmetric and positive definite.
All inputs are finite; a program needn't handle non-finite values.
Results may differ from a plain program's by a relative error of at most 0.00019.
Values sent between devices are 32-bit elements; how exact they have to be, the bound alone decides.
No kernel may reach another device: no remote copies, remote signals or barrier semaphores. Data moves between devices by JAX's collectives and lax.ppermute only.
A program may use at most 64 MiB of HBM per device.

v0:
```python
import jax
import jax.numpy as jnp
from jax import lax
from jax.sharding import PartitionSpec as P

HIGH = lax.Precision.HIGHEST


def from_partner(block, axis, distance):
    count = lax.axis_size(axis)
    route = []
    for low in range(count):
        high = low | 1 << distance
        if high != low and high < count:
            route += [(low, high), (high, low)]
    return lax.ppermute(block, axis, route)


def gram_of(left, right):
    return lax.dot_general(
        left, right, (((0,), (0,)), ((), ())), precision=HIGH, preferred_element_type=jnp.float32
    )


def times_matrix(left, right):
    return jnp.dot(left, right, precision=HIGH, preferred_element_type=jnp.float32)


def definite_solve(matrix, target):
    factor = jnp.linalg.cholesky(matrix)
    lower_part = lax.linalg.triangular_solve(factor, target, left_side=True, lower=True)
    return lax.linalg.triangular_solve(
        factor, lower_part, left_side=True, lower=True, transpose_a=True
    )


def half_sums(local_terms):
    summed = lax.psum(local_terms, "leaf")
    return summed + from_partner(summed, "group", 0)


def per_device(q_two, q_one, sources, coupling_two, coupling_one):
    panel_width = q_two.shape[1]
    half_index = lax.axis_index("group") // 2
    coupling = lax.dynamic_index_in_dim(coupling_two, half_index, 0, keepdims=False)
    level_terms = [gram_of(q_two, q_two), gram_of(q_two, q_one), gram_of(q_two, sources)]
    summed = half_sums(jnp.concatenate(level_terms, axis=1))
    gram_two = summed[:, :panel_width]
    cross = summed[:, panel_width : 2 * panel_width]
    projected = summed[:, 2 * panel_width : 3 * panel_width]
    solved = definite_solve(coupling + gram_two, jnp.concatenate([cross, projected], axis=1))
    update = times_matrix(q_two, solved)
    panel_one = q_one - update[:, :panel_width]
    level_field = sources - update[:, panel_width:]
    top_terms = jnp.concatenate([gram_of(q_one, panel_one), gram_of(q_one, level_field)], axis=1)
    totals = lax.psum(top_terms, ("leaf", "group"))
    weights = definite_solve(coupling_one + totals[:, :panel_width], totals[:, panel_width:])
    solution = level_field - times_matrix(panel_one, weights)
    return (panel_one, solution)


def solution(mesh):
    placed = (
        P(("group", "leaf"), None),
        P(("group", "leaf"), None),
        P(("group", "leaf"), None),
        P(),
        P(),
    )
    return jax.shard_map(
        per_device,
        mesh=mesh,
        in_specs=placed,
        out_specs=(P(("group", "leaf"), None), P(("group", "leaf"), None)),
        check_vma=False,
    )
```

profile of v0, /device:TPU:0, one launch (start us, length us, event | category | flops | bytes accessed | tf_op | source)
XLA Modules:
  0.0 399.4 jit_solution(3324810219155193129)
XLA Ops:
  7.2 1.5 copy-done
  8.8 3.4 fusion.33
  12.2 3.6 fusion.34
  15.9 3.6 fusion.35
  19.5 0.9 pad_maximum_fusion
  20.5 0.3 all-reduce.6.cloned.1.call-start
  20.8 77.3 %all-reduce.4.cloned.1.call-done = f32[256,768]{0,1:T(8,128)} async-done(((f32[256,768]{0,1:T(8,128)}), f32[256,768]{0,1:T(8,128)}) %all-reduce.4.cloned.1.call-update) | async-done | bytes 786448 | tf_op jit(solution)/shard_map/psum | solution.py:38
  98.1 2.9 copy.10
  101.0 2.9 copy.9
  103.9 0.1 copy.7
  104.1 1.5 add.43
  105.6 0.1 copy.8
  105.8 0.7 copy-done.9
  106.5 11.7 %cholesky.130 = f32[128,128]{1,0:T(8,128)S(1)} custom-call(f32[128,128]{1,0:T(8,128)S(1)} %cholesky.194), custom_call_target="Cholesky" | custom-call | tf_op jit(solution)/shard_map/jit(cholesky)/cholesky | solution.py:30
  118.3 9.8 %custom-call.21 = f32[1,128,128]{1,2,0:T(8,128)S(1)} custom-call(f32[1,128,128]{2,1,0:T(8,128)S(1)} %get-tuple-element.48), custom_call_target="InvertDiagBlocksLowerTriangular" | custom-call | tf_op jit(solution)/shard_map/jit(cholesky)/cholesky | solution.py:30
  128.1 1.0 constant_dynamic-update-slice_fusion.3
  129.1 1.1 convolution_subtract_fusion.5
  130.3 11.7 %cholesky.147 = f32[128,128]{1,0:T(8,128)S(1)} custom-call(f32[128,128]{1,0:T(8,128)S(1)} %convolution_subtract_fusion.5), custom_call_target="Cholesky" | custom-call | tf_op jit(solution)/shard_map/jit(cholesky)/cholesky | solution.py:30
  142.0 0.7 compare_reduce_fusion.2
  144.1 4.0 while.2
  144.1 0.6 fusion.62
  144.7 1.4 bitcast_dynamic-update-slice_fusion.4
  146.1 0.6 fusion.62
  146.7 1.4 bitcast_dynamic-update-slice_fusion.4
  148.1 28.4 %custom-call.18 = f32[2,128,128]{1,2,0:T(8,128)S(1)} custom-call(f32[2,128,128]{2,1,0:T(8,128)S(1)} %get-tuple-element.10), custom_call_target="InvertDiagBlocksLowerTriangular" | custom-call | tf_op jit(solution)/shard_map/triangular_solve | solution.py:32
  176.5 0.4 fusion.4
  176.9 0.6 fusion.27
  177.5 0.4 fusion.3
  178.0 0.4 fusion.20
  178.3 0.4 convolution_subtract_fusion.1
  178.8 0.4 fusion.19
  179.2 7.0 %convolution_bitcast_fusion = f32[2048,512]{0,1:T(8,128)S(1)} fusion(f32[2048,256]{1,0:T(8,128)S(1)} %copy-done, f32[128,512]{1,0:T(8,128)S(1)} %fusion.20, f32[128,512]{1,0:T(8,128)S(1)} %fusion.19), kind=kOutput, calls=%fused_computation.4 | convolution fusion | flops 3221356544 | bytes 6815744 | tf_op jit(solution)/shard_map/dot_general | solution.py:26
  186.2 2.0 convolution_bitcast_fusion.1
  188.2 0.1 copy-done.5
  188.3 1.0 copy-done.7
  189.3 0.3 slice_subtract_fusion.1
  189.7 2.1 convolution_bitcast_fusion.2
  191.8 0.8 pad_maximum_fusion.1
  192.7 0.1 copy.11
  192.8 2.9 copy.14
  195.7 124.2 %all-reduce.6.cloned.1.call-done = f32[256,512]{0,1:T(8,128)} async-done(((f32[256,512]{0,1:T(8,128)}), f32[256,512]{0,1:T(8,128)}) %all-reduce.6.cloned.1.call-update) | async-done | bytes 524304 | tf_op jit(solution)/shard_map/psum | solution.py:56
  319.9 1.0 slice_add_fusion
  320.9 0.1 copy.12
  321.1 11.7 %cholesky.164 = f32[128,128]{1,0:T(8,128)S(1)} custom-call(f32[128,128]{1,0:T(8,128)S(1)} %cholesky.197), custom_call_target="Cholesky" | custom-call | tf_op jit(solution)/shard_map/jit(cholesky)/cholesky | solution.py:30
  332.9 9.8 %custom-call.22 = f32[1,128,128]{1,2,0:T(8,128)S(1)} custom-call(f32[1,128,128]{2,1,0:T(8,128)S(1)} %get-tuple-element.44), custom_call_target="InvertDiagBlocksLowerTriangular" | custom-call | tf_op jit(solution)/shard_map/jit(cholesky)/cholesky | solution.py:30
  342.7 0.2 constant_dynamic-update-slice_fusion.1
  342.9 0.3 convolution_subtract_fusion.4
  343.2 11.7 %cholesky.181 = f32[128,128]{1,0:T(8,128)S(1)} custom-call(f32[128,128]{1,0:T(8,128)S(1)} %convolution_subtract_fusion.4), custom_call_target="Cholesky" | custom-call | tf_op jit(solution)/shard_map/jit(cholesky)/cholesky | solution.py:30
  355.0 0.7 compare_reduce_fusion
  355.6 0.7 compare_reduce_fusion.1
  357.6 4.0 %while.3 = (s32[]{:T(128)}, f32[256,256]{1,0:T(8,128)S(1)}, s32[2,2]{1,0:T(2,128)S(1)}, f32[2,128,128]{2,1,0:T(8,128)S(1)}, s32[]{:T(128)}) while((s32[]{:T(128)}, f32[256,256]{1,0:T(8,128)S(1)}, s32[2,2]{1,0:T(2,128)S(1)}, f32[2,128,128]{2,1,0:T(8,128)S(1)}, s32[]{:T(128)}) %tuple.56), condition=%wide.while_cond.1, body=%wide.while_body.1.sunk | while | flops 2 | bytes 131181 | solution.py:32
  357.6 0.6 fusion.63
  358.3 1.3 bitcast_dynamic-update-slice_fusion.5
  359.7 0.6 fusion.63
  360.3 1.3 bitcast_dynamic-update-slice_fusion.5
  361.6 19.9 %custom-call.19 = f32[2,128,128]{1,2,0:T(8,128)S(1)} custom-call(f32[2,128,128]{2,1,0:T(8,128)S(1)} %get-tuple-element.18), custom_call_target="InvertDiagBlocksLowerTriangular" | custom-call | tf_op jit(solution)/shard_map/triangular_solve | solution.py:32
  381.6 0.3 fusion.11
  381.9 0.4 convolution_subtract_fusion.3
  382.3 0.3 fusion.23
  382.6 0.3 fusion.22
  382.9 0.3 convolution_subtract_fusion.2
  383.2 0.3 fusion.21
  383.5 5.7 %convolution_subtract_fusion = f32[2048,256]{0,1:T(8,128)} fusion(f32[2048,256]{0,1:T(8,128)S(1)} %copy-done.4, f32[2048,256]{0,1:T(8,128)} %copy.10, f32[2048,512]{0,1:T(8,128)} %copy-done.5, f32[128,256]{1,0:T(8,128)S(1)} %fusion.22, f32[128,256]{1,0:T(8,128)S(1)} %fusion.21), kind=kOutput, calls=%fused_computation.5 | convolution fusion | flops 1611726848 | bytes 8650752 | tf_op jit(solution)/shard_map/dot_general | solution.py:26
  389.2 2.9 copy.15
  (49 shorter events, 0.6 us)
Async XLA Ops:
  7.2 1.6 copy-start
  7.2 90.9 %all-reduce.4.cloned.1.call-start = ((), (), s32[]{:S(2)}) async-start(), calls=%async_computation | async-start | bytes 1572864 | tf_op jit(solution)/shard_map/psum | solution.py:38
  8.8 3.5 copy-start.1
  12.2 3.7 copy-start.8
  20.5 299.5 %all-reduce.6.cloned.1.call-start = ((), (), s32[]{:S(2)}) async-start(), calls=%async_computation.1 | async-start | bytes 1048576 | tf_op jit(solution)/shard_map/psum | solution.py:56
  98.0 6.0 %collective-permute-start = (f32[256,768]{0,1:T(8,128)}, f32[256,768]{0,1:T(8,128)}, u32[]{:S(2)}, u32[]{:S(2)}) collective-permute-start(f32[256,768]{0,1:T(8,128)} %all-reduce.4.cloned.1.call-done), channel_id=1, source_target_pairs={{0,1},{1,0},{2,3},{3,2},{4,5},{5,4},{6,7},{7,6},{8,9},{9,8},{10,11... | collective-permute-start | bytes 2359304 | tf_op jit(solution)/shard_map/ppermute | solution.py:16
  101.0 2.9 copy-start.12
  105.8 0.7 copy-start.9
  179.1 7.0 %copy-start.2 = (f32[2048,256]{1,0:T(8,128)S(1)}, f32[2048,256]{1,0:T(8,128)}, u32[]{:S(2)}) copy-start(f32[2048,256]{1,0:T(8,128)} %param.7) | copy-start | bytes 6291460
  179.2 7.0 %copy-start.6 = (f32[2048,256]{0,1:T(8,128)S(1)}, f32[2048,256]{0,1:T(8,128)}, u32[]{:S(2)}) copy-start(f32[2048,256]{0,1:T(8,128)} %copy.10) | copy-start | bytes 6291460
  186.2 2.1 copy-start.5
  186.2 3.1 copy-start.7
  189.7 2.2 copy-start.3
  189.7 3.0 copy-start.11
  320.9 60.7 %copy-start.10 = (f32[256,512]{0,1:T(8,128)S(1)}, f32[256,512]{0,1:T(8,128)}, u32[]{:S(2)}) copy-start(f32[256,512]{0,1:T(8,128)} %all-reduce.6.cloned.1.call-done) | copy-start | bytes 1572868
  381.6 1.9 copy-start.4
Sparse Core Ops, SparseCore 0:
  20.6 77.3 all-reduce.3
  192.8 127.0 all-reduce.5
where the time goes:
time: 408 us; the launch traced here: 399 us
  waiting for transfers between devices  202 us (50%)
  other arithmetic  122 us (30%)
  matrix products  34.6 us (8%)
  local copies, waits for them, and re-layouts  23.6 us (6%)
  between operations  17.5 us (4%)
    psum x1, waiting for transfers between devices, per_device(): totals = lax.psum(top_terms, ('leaf', 'group'))  124 us
    psum x1, waiting for transfers between devices, half_sums(): summed = lax.psum(local_terms, 'leaf')  77.3 us
    another operation x13, other arithmetic, definite_solve(): factor = jnp.linalg.cholesky(matrix)  68.6 us
    another operation x5, other arithmetic, definite_solve(): lax.linalg.triangular_solve(factor, lower_part, left_side=True, lower=Tru...  48.4 us
    unnamed x33, local copies, waits for them, and re-layouts  15.2 us
    dot_general x5, matrix products, gram_of(): lax.dot_general(left, right, (((0,), (0,)), ((), ())), precision=HIGH, pr...  14.8 us
    dot_general x2, matrix products, times_matrix(): jnp.dot(left, right, precision=HIGH, preferred_element_type=jnp.float32)  12.7 us
  transfers between devices with their start and end apart: 3, of which 2 were waited for; matrix products, arithmetic and copies ran while one was open for 2% of the time, Pallas kernels for 0%

commit v1 on v0

v1 whole, which is shorter than its diff:
```python
import functools

import jax
import jax.numpy as jnp
from jax import lax
from jax.experimental import pallas as pl
from jax.experimental.pallas import tpu as pltpu
from jax.sharding import PartitionSpec as P

HIGH = lax.Precision.HIGHEST
AXES = ("leaf", "group")
F32 = jnp.float32
BF16 = jnp.bfloat16
R = 256
LANES = 128
PANEL = 32
TILE = 512
VMEM_LIMIT = 40 * 1024 * 1024
TERMS = 2304
TOP = 896


def split2(x):
    high = x.astype(BF16)
    return high, (x - high.astype(F32)).astype(BF16)


def split3(x):
    high = x.astype(BF16)
    rest = x - high.astype(F32)
    mid = rest.astype(BF16)
    return high, mid, (rest - mid.astype(F32)).astype(BF16)


def dot(left, right):
    return jnp.dot(left, right, preferred_element_type=F32)


def dot_t(left, right):
    return lax.dot_general(left, right, (((0,), (0,)), ((), ())), preferred_element_type=F32)


def dot_full(left, right):
    return jnp.dot(left, right, precision=HIGH, preferred_element_type=F32)


def dot_t_full(left, right):
    return lax.dot_general(
        left, right, (((0,), (0,)), ((), ())), precision=HIGH, preferred_element_type=F32
    )


def store_symmetric(ref, row, block):
    ref[row : row + 128, :] = block[:128, :128]
    ref[row + 128 : row + 256, :] = block[128:, :128]
    ref[row + 256 : row + 384, :] = block[128:, 128:]


def store_square(ref, row, block):
    ref[row : row + 256, :] = block[:, :128]
    ref[row + 256 : row + 512, :] = block[:, 128:]


def load_symmetric(ref, row):
    lower = ref[row + 128 : row + 256, :]
    top = jnp.concatenate([ref[row : row + 128, :], lower.T], axis=1)
    bottom = jnp.concatenate([lower, ref[row + 256 : row + 384, :]], axis=1)
    return jnp.concatenate([top, bottom], axis=0)


def load_square(ref, row):
    return jnp.concatenate([ref[row : row + 256, :], ref[row + 256 : row + 512, :]], axis=1)


def gram_kernel(q_two, q_one, sources, out, acc):
    step = pl.program_id(0)

    @pl.when(step == 0)
    def _():
        acc[...] = jnp.zeros_like(acc)

    h2, l2 = split2(q_two[...])
    h1, l1 = split2(q_one[...])
    hs, ls = split2(sources[...])
    acc[0] += dot_t(h2, h2)
    acc[1] += dot_t(h2, l2)
    acc[2] += dot_t(h2, h1) + dot_t(h2, l1) + dot_t(l2, h1)
    acc[3] += dot_t(h2, hs) + dot_t(h2, ls) + dot_t(l2, hs)
    acc[4] += dot_t(h1, h1)
    acc[5] += dot_t(h1, l1)
    acc[6] += dot_t(h1, hs) + dot_t(h1, ls) + dot_t(l1, hs)

    @pl.when(step == pl.num_programs(0) - 1)
    def _():
        cross2 = acc[1]
        store_symmetric(out, 0, acc[0] + cross2 + cross2.T)
        store_square(out, 384, acc[2])
        store_square(out, 896, acc[3])
        cross1 = acc[5]
        store_symmetric(out, 1408, acc[4] + cross1 + cross1.T)
        store_square(out, 1792, acc[6])


def gram_terms(q_two, q_one, sources):
    rows = q_two.shape[0]
    spec = pl.BlockSpec((TILE, R), lambda i: (i, 0))
    return pl.pallas_call(
        gram_kernel,
        grid=(rows // TILE,),
        in_specs=[spec, spec, spec],
        out_specs=pl.BlockSpec((TERMS, LANES), lambda i: (0, 0)),
        out_shape=jax.ShapeDtypeStruct((TERMS, LANES), F32),
        scratch_shapes=[pltpu.VMEM((7, R, R), F32)],
        compiler_params=pltpu.CompilerParams(vmem_limit_bytes=VMEM_LIMIT),
        name="gram",
    )(q_two, q_one, sources)


def spread_lane(x, lane):
    return jnp.broadcast_to(x[:, lane : lane + 1], (8, LANES))


def spread_row(x, row):
    return jnp.broadcast_to(x[row : row + 1, :], (8, LANES))


def reciprocal(x):
    y = pl.reciprocal(x, approx=True)
    y = y * (2.0 - x * y)
    return y * (2.0 - x * y)


def eliminate(diag, rows):
    lane = lax.broadcasted_iota(jnp.int32, (8, LANES), 1)
    sub = lax.broadcasted_iota(jnp.int32, (8, LANES), 0)
    for k in range(0, PANEL, 2):
        at, s = k // 8, k % 8
        c1 = [spread_lane(d, k) for d in diag]
        c2 = [spread_lane(d, k + 1) for d in diag]
        a = spread_row(c1[at], s)
        b = spread_row(c1[at], s + 1)
        c = spread_row(c2[at], s + 1)
        inv = reciprocal(a * c - b * b)
        e, f, g = c * inv, b * inv, a * inv
        first, second = lane == k, lane == k + 1
        either = first | second
        r1 = jnp.where(first, 1.0, jnp.where(second, 0.0, spread_row(diag[at], s)))
        r2 = jnp.where(first, 0.0, jnp.where(second, 1.0, spread_row(diag[at], s + 1)))
        p1 = [spread_row(x, s) for x in rows[at]]
        p2 = [spread_row(x, s + 1) for x in rows[at]]
        n1, n2 = e * r1 - f * r2, g * r2 - f * r1
        m1 = [e * x - f * y for x, y in zip(p1, p2)]
        m2 = [g * y - f * x for x, y in zip(p1, p2)]
        for i in range(4):
            base = jnp.where(either, 0.0, diag[i])
            x = list(rows[i])
            u, v = c1[i], c2[i]
            if i == at:
                own1, own2 = sub == s, sub == s + 1
                own = own1 | own2
                base = jnp.where(own, 0.0, base)
                x = [jnp.where(own, 0.0, y) for y in x]
                u = jnp.where(own1, -1.0, jnp.where(own2, 0.0, u))
                v = jnp.where(own2, -1.0, jnp.where(own1, 0.0, v))
            diag[i] = base - u * n1 - v * n2
            rows[i] = [y - u * m - v * n for y, m, n in zip(x, m1, m2)]
    return diag, rows


def stack_left(x):
    h, m, l = split3(x)
    return jnp.concatenate([h, h, m, h, l, m], axis=0)


def stack_right(x):
    h, m, l = split3(x)
    return jnp.concatenate([h, m, h, l, h, m], axis=0)


def invert(matrix, work):
    eye = lax.broadcasted_iota(jnp.int32, (R, R), 0) == lax.broadcasted_iota(jnp.int32, (R, R), 1)
    diagonal = jnp.where(eye, matrix, 0.0)
    scale_row = lax.rsqrt(jnp.sum(diagonal, axis=0, keepdims=True))
    scale_col = lax.rsqrt(jnp.sum(diagonal, axis=1, keepdims=True))
    work[...] = matrix * scale_col * scale_row
    lanes = lax.broadcasted_iota(jnp.int32, (PANEL, R), 1)
    lanes_all = lax.broadcasted_iota(jnp.int32, (R, R), 1)

    def sweep(j, carry):
        start = pl.multiple_of(j * PANEL, PANEL)
        panel = work[pl.ds(start, PANEL), :]
        shift = lax.rem(j, 4) * PANEL
        half = jnp.where(j < 4, panel[:, :LANES], panel[:, LANES:])
        diag = pltpu.roll(half, lax.rem(LANES - shift, LANES), axis=1)
        diag_parts = [diag[8 * i : 8 * i + 8, :] for i in range(4)]
        row_parts = [
            [panel[8 * i : 8 * i + 8, :LANES], panel[8 * i : 8 * i + 8, LANES:]] for i in range(4)
        ]
        diag_parts, row_parts = eliminate(diag_parts, row_parts)
        inverse = pltpu.roll(jnp.concatenate(diag_parts, axis=0), shift, axis=1)
        inverse = jnp.concatenate([inverse, inverse], axis=1)
        product = jnp.concatenate([jnp.concatenate(x, axis=1) for x in row_parts], axis=0)
        inside = (lanes >= start) & (lanes < start + PANEL)
        swept = jnp.where(inside, -inverse, product)
        change = dot_t(stack_left(panel), stack_right(swept))
        inside_all = (lanes_all >= start) & (lanes_all < start + PANEL)
        work[...] = jnp.where(inside_all, 0.0, work[...]) - change
        work[pl.ds(start, PANEL), :] = swept
        return carry

    lax.fori_loop(0, R // PANEL, sweep, 0)
    return -(work[...] * scale_col * scale_row)


def level_kernel(terms, coupling, x_out, y_out, top_out, work):
    half = lax.axis_index("group") // 2
    inverse = invert(coupling[half] + load_symmetric(terms, 0), work)
    cross = load_square(terms, 384)
    x = dot_full(inverse, cross)
    y = dot_full(inverse, load_square(terms, 896))
    x_out[...] = x
    y_out[...] = y
    store_symmetric(top_out, 0, load_symmetric(terms, 1408) - dot_t_full(cross, x))
    store_square(top_out, 384, load_square(terms, 1792) - dot_t_full(cross, y))


def level_solve(terms, coupling):
    square = jax.ShapeDtypeStruct((R, R), F32)
    return pl.pallas_call(
        level_kernel,
        out_shape=(square, square, jax.ShapeDtypeStruct((TOP, LANES), F32)),
        scratch_shapes=[pltpu.VMEM((R, R), F32)],
        compiler_params=pltpu.CompilerParams(vmem_limit_bytes=VMEM_LIMIT),
        name="level_solve",
    )(terms, coupling)


def root_kernel(top, coupling, x, y, w_out, z_out, work):
    inverse = invert(coupling[...] + load_symmetric(top, 0), work)
    w = dot_full(inverse, load_square(top, 384))
    w_out[...] = w
    z_out[...] = y[...] - dot_full(x[...], w)


def root_solve(top, coupling, x, y):
    square = jax.ShapeDtypeStruct((R, R), F32)
    return pl.pallas_call(
        root_kernel,
        out_shape=(square, square),
        scratch_shapes=[pltpu.VMEM((R, R), F32)],
        compiler_params=pltpu.CompilerParams(vmem_limit_bytes=VMEM_LIMIT),
        name="root_solve",
    )(top, coupling, x, y)


def dot_three(lh, ll, rh, rl):
    return dot(lh, rh) + (dot(lh, rl) + dot(ll, rh))


def panel_kernel(q_two, q_one, x, out):
    out[...] = q_one[...] - dot_three(*split2(q_two[...]), *split2(x[...]))


def field_kernel(q_two, q_one, sources, w, z, out):
    change = dot_three(*split2(q_one[...]), *split2(w[...]))
    change += dot_three(*split2(q_two[...]), *split2(z[...]))
    out[...] = sources[...] - change


def update(kernel, tall, square, name):
    rows = tall[0].shape[0]
    spec = pl.BlockSpec((TILE, R), lambda i: (i, 0))
    whole = pl.BlockSpec((R, R), lambda i: (0, 0))
    return pl.pallas_call(
        kernel,
        grid=(rows // TILE,),
        in_specs=[spec] * len(tall) + [whole] * len(square),
        out_specs=spec,
        out_shape=jax.ShapeDtypeStruct((rows, R), F32),
        compiler_params=pltpu.CompilerParams(vmem_limit_bytes=VMEM_LIMIT),
        name=name,
    )(*tall, *square)


def exchange(x, mask):
    count = lax.axis_size(AXES)
    return lax.ppermute(x, AXES, [(i, i ^ mask) for i in range(count)])


def code_of(index, bits):
    code = 0
    for place, bit in enumerate(bits):
        code = code | ((index >> bit) & 1) << place
    return code


def mask_of(code, bits):
    return sum(1 << bit for place, bit in enumerate(bits) if code >> place & 1)


def reduce_scatter(x, index, bits):
    count = 1 << len(bits)
    mine = code_of(index, bits)
    parts = x.reshape(count, x.shape[0] // count, x.shape[1])
    got = lax.dynamic_index_in_dim(parts, mine, 0, keepdims=False)
    arrived = []
    for other in range(1, count):
        part = lax.dynamic_index_in_dim(parts, mine ^ other, 0, keepdims=False)
        arrived.append(exchange(part, mask_of(other, bits)))
    for part in arrived:
        got = got + part
    return got


def all_gather(x, index, bits):
    count = 1 << len(bits)
    mine = code_of(index, bits)
    pieces = [x] + [exchange(x, mask_of(other, bits)) for other in range(1, count)]
    out = jnp.zeros((count,) + x.shape, x.dtype)
    for other, piece in enumerate(pieces):
        out = lax.dynamic_update_index_in_dim(out, piece, mine ^ other, 0)
    return out.reshape(count * x.shape[0], x.shape[1])


def per_device(q_two, q_one, sources, coupling_two, coupling_one):
    leaf_bits = lax.axis_size("leaf").bit_length() - 1
    index = lax.axis_index(AXES)
    stages = [[0]]
    for low in range(2, leaf_bits + 2, 3):
        stages.append(list(range(low, min(low + 3, leaf_bits + 2))))
    terms = gram_terms(q_two, q_one, sources)
    for bits in stages:
        terms = reduce_scatter(terms, index, bits)
    for bits in reversed(stages):
        terms = all_gather(terms, index, bits)
    x, y, top = level_solve(terms, coupling_two)
    mine = index & 1
    parts = top.reshape(2, TOP // 2, LANES)
    part = lax.dynamic_index_in_dim(parts, mine, 0, keepdims=False)
    part = part + exchange(part, 2)
    top = all_gather(part, index, [0])
    panel_one = update(panel_kernel, [q_two, q_one], [x], "panel")
    w, z = root_solve(top, coupling_one, x, y)
    solution = update(field_kernel, [q_two, q_one, sources], [w, z], "field")
    return (panel_one, solution)


def solution(mesh):
    placed = P(("group", "leaf"), None)
    return jax.shard_map(
        per_device,
        mesh=mesh,
        in_specs=(placed, placed, placed, P(), P()),
        out_specs=(placed, placed),
        check_vma=False,
    )
```

time: 408 us -> 117 us (0.29); the launches traced: 399 us -> 116 us
  waiting for transfers between devices: 202 us -> 26.6 us
  other arithmetic: 122 us -> 0.15 us
  Pallas kernels: 0 us -> 56.3 us
  matrix products: 34.6 us -> 0 us
  starting transfers between devices: 0.34 us -> 27.2 us
  local copies, waits for them, and re-layouts: 23.6 us -> 5.25 us
  between operations: 17.5 us -> 0.93 us
    psum x2 -> x0, waiting for transfers between devices: 201 us -> none  [the longest x1 124 us: per_device(): totals = lax.psum(top_terms, ('leaf', 'group'))]
    another operation x18 -> x0, other arithmetic: 117 us -> none  [the longest x13 68.6 us: definite_solve(): factor = jnp.linalg.cholesky(matrix)]
    pallas_call x0 -> x5, Pallas kernels: none -> 56.3 us  [the longest x1 22.8 us: level_solve(): pl.pallas_call(level_kernel, out_shape=(square, square, jax.ShapeDtypeStr...]
    dot_general x7 -> x0, matrix products: 27.5 us -> none  [the longest x5 14.8 us: gram_of(): lax.dot_general(left, right, (((0,), (0,)), ((), ())), precision=HIGH, pr...]
    ppermute x1 -> x18, starting transfers between devices: 0.01 us -> 27.2 us  [exchange(): return lax.ppermute(x, AXES, [(i, i ^ mask) for i in range(count)])]
    ppermute x1 -> x18, waiting for transfers between devices: 0.01 us -> 26.6 us  [exchange(): return lax.ppermute(x, AXES, [(i, i ^ mask) for i in range(count)])]
    unnamed x33 -> x16, local copies, waits for them, and re-layouts: 15.2 us -> 4.8 us
    another operation x17 -> x0, local copies, waits for them, and re-layouts: 8.02 us -> none
  transfers between devices with their start and end apart: 3 -> 18, of which waited for: 2 -> 6; matrix products, arithmetic and copies ran while one was open for 2% -> 0% of each run, Pallas kernels for 0% -> 2%
where the time goes in v1:
time: 117 us; the launch traced here: 116 us
  Pallas kernels  56.3 us (48%)
  starting transfers between devices  27.2 us (23%)
  waiting for transfers between devices  26.6 us (23%)
  local copies, waits for them, and re-layouts  5.25 us (4%)
    ppermute x18, starting transfers between devices, exchange(): return lax.ppermute(x, AXES, [(i, i ^ mask) for i in range(count)])  27.2 us
    ppermute x18, waiting for transfers between devices, exchange(): return lax.ppermute(x, AXES, [(i, i ^ mask) for i in range(count)])  26.6 us
    pallas_call x1, Pallas kernels, level_solve(): pl.pallas_call(level_kernel, out_shape=(square, square, jax.ShapeDtypeStr...  22.8 us
    pallas_call x1, Pallas kernels, root_solve(): pl.pallas_call(root_kernel, out_shape=(square, square), scratch_shapes=[p...  22.6 us
    pallas_call x2, Pallas kernels, update(): pl.pallas_call(kernel, grid=(rows // TILE,), in_specs=[spec] * len(tall)...  6.17 us
    unnamed x16, local copies, waits for them, and re-layouts  4.8 us
    pallas_call x1, Pallas kernels, gram_terms(): pl.pallas_call(gram_kernel, grid=(rows // TILE,), in_specs=[spec, spec, s...  4.71 us
  transfers between devices with their start and end apart: 18, of which 6 were waited for; matrix products, arithmetic and copies ran while one was open for 0% of the time, Pallas kernels for 2%

profile of v1, /device:TPU:0, one launch (start us, length us, event | category | flops | bytes accessed | tf_op | source)
XLA Modules:
  0.0 116.5 jit_solution(16917915992545042677)
XLA Ops:
  0.6 0.0 copy-start
  0.7 1.6 %copy-done = f32[2048,256]{1,0:T(8,128)S(1)} copy-done((f32[2048,256]{1,0:T(8,128)S(1)}, f32[2048,256]{1,0:T(8,128)}, u32[]{:S(2)}) %copy-start) | copy-done | bytes 2097176
  2.2 0.0 copy-start.2
  2.2 1.6 %copy-done.2 = f32[2048,256]{1,0:T(8,128)S(1)} copy-done((f32[2048,256]{1,0:T(8,128)S(1)}, f32[2048,256]{1,0:T(8,128)}, u32[]{:S(2)}) %copy-start.2) | copy-done | bytes 2097176
  3.8 0.0 copy-start.4
  3.8 1.6 %copy-done.4 = f32[2048,256]{1,0:T(8,128)S(1)} copy-done((f32[2048,256]{1,0:T(8,128)S(1)}, f32[2048,256]{1,0:T(8,128)}, u32[]{:S(2)}) %copy-start.4) | copy-done | bytes 2097176
  5.4 4.7 %gram.1 = f32[2304,128]{1,0:T(8,128)S(1)} custom-call(f32[2048,256]{1,0:T(8,128)S(1)} %copy-done, f32[2048,256]{1,0:T(8,128)S(1)} %copy-done.2, f32[2048,256]{1,0:T(8,128)S(1)} %copy-done.4), custom_call_target="tpu_custom_call" | custom-call | tf_op jit(solution)/shard_map/gram/pallas_call | solution.py:107
  10.2 0.5 collective-permute-start
  10.7 1.6 %collective-permute-done = f32[1152,128]{1,0:T(8,128)S(1)} collective-permute-done((f32[1152,128]{1,0:T(8,128)S(1)}, f32[1152,128]{1,0:T(8,128)S(1)}, u32[]{:S(2)}, u32[]{:S(2)}) %collective-permute-start) | collective-permute-done | bytes 589856 | tf_op jit(solution)/shard_map/ppermute | solution.py:287
  12.3 0.1 bitcast_add_fusion
  12.4 0.1 dynamic-slice_bitcast_fusion.8
  12.5 2.9 %collective-permute-start.1 = (f32[144,128]{1,0:T(8,128)S(1)}, f32[144,128]{1,0:T(8,128)S(1)}, u32[]{:S(2)}, u32[]{:S(2)}) collective-permute-start(f32[144,128]{1,0:T(8,128)S(1)} %get-tuple-element.16), channel_id=1, source_target_pairs={{0,4},{1,5},{2,6},{3,7},{4,0},{5,1},{6,2},{7,3},{8,12},{9,13},{10,... | collective-permute-start | bytes 221192 | tf_op jit(solution)/shard_map/ppermute | solution.py:287
  15.4 3.6 %collective-permute-start.7 = (f32[144,128]{1,0:T(8,128)S(1)}, f32[144,128]{1,0:T(8,128)S(1)}, u32[]{:S(2)}, u32[]{:S(2)}) collective-permute-start(f32[144,128]{1,0:T(8,128)S(1)} %get-tuple-element.17), channel_id=1, source_target_pairs={{0,28},{1,29},{2,30},{3,31},{4,24},{5,25},{6,26},{7,27},{8,20},{9,... | collective-permute-start | bytes 221192 | tf_op jit(solution)/shard_map/ppermute | solution.py:287
  19.0 0.0 collective-permute-start.6
  19.0 1.9 %collective-permute-start.5 = (f32[144,128]{1,0:T(8,128)S(1)}, f32[144,128]{1,0:T(8,128)S(1)}, u32[]{:S(2)}, u32[]{:S(2)}) collective-permute-start(f32[144,128]{1,0:T(8,128)S(1)} %get-tuple-element.19), channel_id=1, source_target_pairs={{0,20},{1,21},{2,22},{3,23},{4,16},{5,17},{6,18},{7,19},{8,28},{9,... | collective-permute-start | bytes 221192 | tf_op jit(solution)/shard_map/ppermute | solution.py:287
  20.9 2.1 %collective-permute-start.4 = (f32[144,128]{1,0:T(8,128)S(1)}, f32[144,128]{1,0:T(8,128)S(1)}, u32[]{:S(2)}, u32[]{:S(2)}) collective-permute-start(f32[144,128]{1,0:T(8,128)S(1)} %get-tuple-element.20), channel_id=1, source_target_pairs={{0,16},{1,17},{2,18},{3,19},{4,20},{5,21},{6,22},{7,23},{8,24},{9,... | collective-permute-start | bytes 221192 | tf_op jit(solution)/shard_map/ppermute | solution.py:287
  23.0 0.0 collective-permute-done.1
  23.0 1.2 %collective-permute-start.3 = (f32[144,128]{1,0:T(8,128)S(1)}, f32[144,128]{1,0:T(8,128)S(1)}, u32[]{:S(2)}, u32[]{:S(2)}) collective-permute-start(f32[144,128]{1,0:T(8,128)S(1)} %get-tuple-element.21), channel_id=1, source_target_pairs={{0,12},{1,13},{2,14},{3,15},{4,8},{5,9},{6,10},{7,11},{8,4},{9,5},... | collective-permute-start | bytes 221192 | tf_op jit(solution)/shard_map/ppermute | solution.py:287
  24.3 0.0 collective-permute-done.7
  24.3 2.4 %collective-permute-start.2 = (f32[144,128]{1,0:T(8,128)S(1)}, f32[144,128]{1,0:T(8,128)S(1)}, u32[]{:S(2)}, u32[]{:S(2)}) collective-permute-start(f32[144,128]{1,0:T(8,128)S(1)} %get-tuple-element.22), channel_id=1, source_target_pairs={{0,8},{1,9},{2,10},{3,11},{4,12},{5,13},{6,14},{7,15},{8,0},{9,1},... | collective-permute-start | bytes 221192 | tf_op jit(solution)/shard_map/ppermute | solution.py:287
  26.7 0.0 collective-permute-done.6
  26.7 5.0 %collective-permute-done.5 = f32[144,128]{1,0:T(8,128)S(1)} collective-permute-done((f32[144,128]{1,0:T(8,128)S(1)}, f32[144,128]{1,0:T(8,128)S(1)}, u32[]{:S(2)}, u32[]{:S(2)}) %collective-permute-start.5) | collective-permute-done | bytes 73760 | tf_op jit(solution)/shard_map/ppermute | solution.py:287
  31.7 0.0 collective-permute-done.4
  31.7 0.0 collective-permute-done.3
  31.7 0.0 collective-permute-done.2
  31.7 0.1 bitcast_dynamic-update-slice_fusion.11
  31.8 1.5 %collective-permute-start.8 = (f32[144,128]{1,0:T(8,128)S(1)}, f32[144,128]{1,0:T(8,128)S(1)}, u32[]{:S(2)}, u32[]{:S(2)}) collective-permute-start(f32[144,128]{1,0:T(8,128)S(1)} %get-tuple-element.15), channel_id=1, source_target_pairs={{0,4},{1,5},{2,6},{3,7},{4,0},{5,1},{6,2},{7,3},{8,12},{9,13},{10,... | collective-permute-start | bytes 221192 | tf_op jit(solution)/shard_map/ppermute | solution.py:287
  33.3 3.1 %collective-permute-start.13 = (f32[144,128]{1,0:T(8,128)S(1)}, f32[144,128]{1,0:T(8,128)S(1)}, u32[]{:S(2)}, u32[]{:S(2)}) collective-permute-start(f32[144,128]{1,0:T(8,128)S(1)} %get-tuple-element.15), channel_id=1, source_target_pairs={{0,24},{1,25},{2,26},{3,27},{4,28},{5,29},{6,30},{7,31},{8,16},{9,... | collective-permute-start | bytes 221192 | tf_op jit(solution)/shard_map/ppermute | solution.py:287
  36.4 0.0 collective-permute-start.12
  36.4 2.9 %collective-permute-start.11 = (f32[144,128]{1,0:T(8,128)S(1)}, f32[144,128]{1,0:T(8,128)S(1)}, u32[]{:S(2)}, u32[]{:S(2)}) collective-permute-start(f32[144,128]{1,0:T(8,128)S(1)} %get-tuple-element.15), channel_id=1, source_target_pairs={{0,16},{1,17},{2,18},{3,19},{4,20},{5,21},{6,22},{7,23},{8,24},{9,... | collective-permute-start | bytes 221192 | tf_op jit(solution)/shard_map/ppermute | solution.py:287
  39.3 0.2 collective-permute-start.10
  39.5 0.0 collective-permute-done.8
  39.5 2.8 %collective-permute-start.9 = (f32[144,128]{1,0:T(8,128)S(1)}, f32[144,128]{1,0:T(8,128)S(1)}, u32[]{:S(2)}, u32[]{:S(2)}) collective-permute-start(f32[144,128]{1,0:T(8,128)S(1)} %get-tuple-element.15), channel_id=1, source_target_pairs={{0,8},{1,9},{2,10},{3,11},{4,12},{5,13},{6,14},{7,15},{8,0},{9,1},... | collective-permute-start | bytes 221192 | tf_op jit(solution)/shard_map/ppermute | solution.py:287
  42.3 5.4 %collective-permute-done.9 = f32[144,128]{1,0:T(8,128)S(1)} collective-permute-done((f32[144,128]{1,0:T(8,128)S(1)}, f32[144,128]{1,0:T(8,128)S(1)}, u32[]{:S(2)}, u32[]{:S(2)}) %collective-permute-start.9) | collective-permute-done | bytes 73760 | tf_op jit(solution)/shard_map/ppermute | solution.py:287
  47.7 0.3 collective-permute-start.14
  48.0 0.0 collective-permute-done.10
  48.0 0.0 collective-permute-done.11
  48.1 0.0 collective-permute-done.12
  48.1 0.0 collective-permute-done.13
  48.1 6.6 %collective-permute-done.14 = f32[144,128]{1,0:T(8,128)S(1)} collective-permute-done((f32[144,128]{1,0:T(8,128)S(1)}, f32[144,128]{1,0:T(8,128)S(1)}, u32[]{:S(2)}, u32[]{:S(2)}) %collective-permute-start.14) | collective-permute-done | bytes 73760 | tf_op jit(solution)/shard_map/ppermute | solution.py:287
  54.7 0.1 collective-permute-start.15
  54.8 0.1 broadcast_in_dim.48
  54.9 0.0 copy-start.6
  55.0 1.8 %collective-permute-done.15 = f32[1152,128]{1,0:T(8,128)S(1)} collective-permute-done((f32[1152,128]{1,0:T(8,128)S(1)}, f32[1152,128]{1,0:T(8,128)S(1)}, u32[]{:S(2)}, u32[]{:S(2)}) %collective-permute-start.15) | collective-permute-done | bytes 589856 | tf_op jit(solution)/shard_map/ppermute | solution.py:287
  56.8 0.0 copy-start.3
  56.9 0.0 copy-done.6
  56.9 0.0 copy-start.1
  56.9 22.8 %level_solve.1 = (f32[256,256]{1,0:T(8,128)S(1)}, f32[256,256]{1,0:T(8,128)S(1)}, f32[896,128]{1,0:T(8,128)S(1)}) custom-call(f32[2304,128]{1,0:T(8,128)S(1)} %bitcast.70, f32[2,256,256]{2,1,0:T(8,128)S(1)} %copy-done.6), custom_call_target="tpu_custom_call" | custom-call | tf_op jit(solution)/shard_map/level_solve/pallas_call | solution.py:229
  79.7 1.6 %collective-permute-start.16 = (f32[448,128]{1,0:T(8,128)S(1)}, f32[448,128]{1,0:T(8,128)S(1)}, u32[]{:S(2)}, u32[]{:S(2)}) collective-permute-start(f32[448,128]{1,0:T(8,128)S(1)} %dynamic-slice_bitcast_fusion.1), channel_id=1, source_target_pairs={{0,2},{1,3},{2,0},{3,1},{4,6},{5,7},{6,4},{7,5},{8,10},{9,11},{10,... | collective-permute-start | bytes 688136 | tf_op jit(solution)/shard_map/ppermute | solution.py:287
  81.3 6.1 %collective-permute-done.16 = f32[448,128]{1,0:T(8,128)S(1)} collective-permute-done((f32[448,128]{1,0:T(8,128)S(1)}, f32[448,128]{1,0:T(8,128)S(1)}, u32[]{:S(2)}, u32[]{:S(2)}) %collective-permute-start.16) | collective-permute-done | bytes 229408 | tf_op jit(solution)/shard_map/ppermute | solution.py:287
  87.5 0.1 collective-permute-start.17
  87.6 0.0 copy-done.3
  87.6 0.0 copy-done.1
  87.6 0.0 copy-start.7
  87.6 0.0 copy-start.5
  87.6 2.8 %panel.1 = f32[2048,256]{1,0:T(8,128)} custom-call(f32[2048,256]{1,0:T(8,128)S(1)} %copy-done.1, f32[2048,256]{1,0:T(8,128)S(1)} %copy-done.3, f32[256,256]{1,0:T(8,128)S(1)} %get-tuple-element.7.x), custom_call_target="tpu_custom_call" | custom-call | tf_op jit(solution)/shard_map/panel/pallas_call | solution.py:274
  90.4 0.0 collective-permute-done.17
  90.4 0.0 copy-done.7
  90.4 22.6 %root_solve.1 = (f32[256,256]{1,0:T(8,128)S(1)}, f32[256,256]{1,0:T(8,128)S(1)}) custom-call(f32[896,128]{1,0:T(8,128)S(1)} %bitcast.71, f32[256,256]{1,0:T(8,128)S(1)} %copy-done.7, f32[256,256]{1,0:T(8,128)S(1)} %get-tuple-element.7.x, f32[256,256]{1,0:T(8,128)S(1)} %get-tuple-element.9.y), custom_call_target="tpu_custom_call" | custom-call | tf_op jit(solution)/shard_map/root_solve/pallas_call | solution.py:247
  113.1 0.0 copy-done.5
  113.1 3.4 %field.1 = f32[2048,256]{1,0:T(8,128)} custom-call(f32[2048,256]{1,0:T(8,128)S(1)} %copy-done.1, f32[2048,256]{1,0:T(8,128)S(1)} %copy-done.3, f32[2048,256]{1,0:T(8,128)S(1)} %copy-done.5, f32[256,256]{1,0:T(8,128)S(1)} %get-tuple-element.10.w, f32[256,256]{1,0:T(8,128)S(1)} %get-tuple-element.11.z), custom_call_target="tpu_custom_call" | custom-call | tf_op jit(solution)/shard_map/field/pallas_call | solution.py:274
  (15 shorter events, 0.4 us)
Async XLA Ops:
  0.6 1.6 %copy-start = (f32[2048,256]{1,0:T(8,128)S(1)}, f32[2048,256]{1,0:T(8,128)}, u32[]{:S(2)}) copy-start(f32[2048,256]{1,0:T(8,128)} %q_two.5) | copy-start | bytes 6291460
  2.2 1.6 %copy-start.2 = (f32[2048,256]{1,0:T(8,128)S(1)}, f32[2048,256]{1,0:T(8,128)}, u32[]{:S(2)}) copy-start(f32[2048,256]{1,0:T(8,128)} %q_one.5) | copy-start | bytes 6291460
  3.8 1.6 %copy-start.4 = (f32[2048,256]{1,0:T(8,128)S(1)}, f32[2048,256]{1,0:T(8,128)}, u32[]{:S(2)}) copy-start(f32[2048,256]{1,0:T(8,128)} %sources.3) | copy-start | bytes 6291460
  10.2 2.1 %collective-permute-start = (f32[1152,128]{1,0:T(8,128)S(1)}, f32[1152,128]{1,0:T(8,128)S(1)}, u32[]{:S(2)}, u32[]{:S(2)}) collective-permute-start(f32[1152,128]{1,0:T(8,128)S(1)} %dynamic-slice_bitcast_fusion), channel_id=1, source_target_pairs={{0,1},{1,0},{2,3},{3,2},{4,5},{5,4},{6,7},{7,6},{8,9},{9,8},{10,11... | collective-permute-start | bytes 1769480 | tf_op jit(solution)/shard_map/ppermute | solution.py:287
  12.5 10.6 %collective-permute-start.1 = (f32[144,128]{1,0:T(8,128)S(1)}, f32[144,128]{1,0:T(8,128)S(1)}, u32[]{:S(2)}, u32[]{:S(2)}) collective-permute-start(f32[144,128]{1,0:T(8,128)S(1)} %get-tuple-element.16), channel_id=1, source_target_pairs={{0,4},{1,5},{2,6},{3,7},{4,0},{5,1},{6,2},{7,3},{8,12},{9,13},{10,... | collective-permute-start | bytes 221192 | tf_op jit(solution)/shard_map/ppermute | solution.py:287
  15.4 8.9 %collective-permute-start.7 = (f32[144,128]{1,0:T(8,128)S(1)}, f32[144,128]{1,0:T(8,128)S(1)}, u32[]{:S(2)}, u32[]{:S(2)}) collective-permute-start(f32[144,128]{1,0:T(8,128)S(1)} %get-tuple-element.17), channel_id=1, source_target_pairs={{0,28},{1,29},{2,30},{3,31},{4,24},{5,25},{6,26},{7,27},{8,20},{9,... | collective-permute-start | bytes 221192 | tf_op jit(solution)/shard_map/ppermute | solution.py:287
  19.0 7.7 %collective-permute-start.6 = (f32[144,128]{1,0:T(8,128)S(1)}, f32[144,128]{1,0:T(8,128)S(1)}, u32[]{:S(2)}, u32[]{:S(2)}) collective-permute-start(f32[144,128]{1,0:T(8,128)S(1)} %get-tuple-element.18), channel_id=1, source_target_pairs={{0,24},{1,25},{2,26},{3,27},{4,28},{5,29},{6,30},{7,31},{8,16},{9,... | collective-permute-start | bytes 221192 | tf_op jit(solution)/shard_map/ppermute | solution.py:287
  19.0 12.7 %collective-permute-start.5 = (f32[144,128]{1,0:T(8,128)S(1)}, f32[144,128]{1,0:T(8,128)S(1)}, u32[]{:S(2)}, u32[]{:S(2)}) collective-permute-start(f32[144,128]{1,0:T(8,128)S(1)} %get-tuple-element.19), channel_id=1, source_target_pairs={{0,20},{1,21},{2,22},{3,23},{4,16},{5,17},{6,18},{7,19},{8,28},{9,... | collective-permute-start | bytes 221192 | tf_op jit(solution)/shard_map/ppermute | solution.py:287
  20.9 10.8 %collective-permute-start.4 = (f32[144,128]{1,0:T(8,128)S(1)}, f32[144,128]{1,0:T(8,128)S(1)}, u32[]{:S(2)}, u32[]{:S(2)}) collective-permute-start(f32[144,128]{1,0:T(8,128)S(1)} %get-tuple-element.20), channel_id=1, source_target_pairs={{0,16},{1,17},{2,18},{3,19},{4,20},{5,21},{6,22},{7,23},{8,24},{9,... | collective-permute-start | bytes 221192 | tf_op jit(solution)/shard_map/ppermute | solution.py:287
  23.0 8.6 %collective-permute-start.3 = (f32[144,128]{1,0:T(8,128)S(1)}, f32[144,128]{1,0:T(8,128)S(1)}, u32[]{:S(2)}, u32[]{:S(2)}) collective-permute-start(f32[144,128]{1,0:T(8,128)S(1)} %get-tuple-element.21), channel_id=1, source_target_pairs={{0,12},{1,13},{2,14},{3,15},{4,8},{5,9},{6,10},{7,11},{8,4},{9,5},... | collective-permute-start | bytes 221192 | tf_op jit(solution)/shard_map/ppermute | solution.py:287
  24.3 7.4 %collective-permute-start.2 = (f32[144,128]{1,0:T(8,128)S(1)}, f32[144,128]{1,0:T(8,128)S(1)}, u32[]{:S(2)}, u32[]{:S(2)}) collective-permute-start(f32[144,128]{1,0:T(8,128)S(1)} %get-tuple-element.22), channel_id=1, source_target_pairs={{0,8},{1,9},{2,10},{3,11},{4,12},{5,13},{6,14},{7,15},{8,0},{9,1},... | collective-permute-start | bytes 221192 | tf_op jit(solution)/shard_map/ppermute | solution.py:287
  31.8 7.7 %collective-permute-start.8 = (f32[144,128]{1,0:T(8,128)S(1)}, f32[144,128]{1,0:T(8,128)S(1)}, u32[]{:S(2)}, u32[]{:S(2)}) collective-permute-start(f32[144,128]{1,0:T(8,128)S(1)} %get-tuple-element.15), channel_id=1, source_target_pairs={{0,4},{1,5},{2,6},{3,7},{4,0},{5,1},{6,2},{7,3},{8,12},{9,13},{10,... | collective-permute-start | bytes 221192 | tf_op jit(solution)/shard_map/ppermute | solution.py:287
  33.3 14.8 %collective-permute-start.13 = (f32[144,128]{1,0:T(8,128)S(1)}, f32[144,128]{1,0:T(8,128)S(1)}, u32[]{:S(2)}, u32[]{:S(2)}) collective-permute-start(f32[144,128]{1,0:T(8,128)S(1)} %get-tuple-element.15), channel_id=1, source_target_pairs={{0,24},{1,25},{2,26},{3,27},{4,28},{5,29},{6,30},{7,31},{8,16},{9,... | collective-permute-start | bytes 221192 | tf_op jit(solution)/shard_map/ppermute | solution.py:287
  36.4 11.7 %collective-permute-start.12 = (f32[144,128]{1,0:T(8,128)S(1)}, f32[144,128]{1,0:T(8,128)S(1)}, u32[]{:S(2)}, u32[]{:S(2)}) collective-permute-start(f32[144,128]{1,0:T(8,128)S(1)} %get-tuple-element.15), channel_id=1, source_target_pairs={{0,20},{1,21},{2,22},{3,23},{4,16},{5,17},{6,18},{7,19},{8,28},{9,... | collective-permute-start | bytes 221192 | tf_op jit(solution)/shard_map/ppermute | solution.py:287
  36.4 11.7 %collective-permute-start.11 = (f32[144,128]{1,0:T(8,128)S(1)}, f32[144,128]{1,0:T(8,128)S(1)}, u32[]{:S(2)}, u32[]{:S(2)}) collective-permute-start(f32[144,128]{1,0:T(8,128)S(1)} %get-tuple-element.15), channel_id=1, source_target_pairs={{0,16},{1,17},{2,18},{3,19},{4,20},{5,21},{6,22},{7,23},{8,24},{9,... | collective-permute-start | bytes 221192 | tf_op jit(solution)/shard_map/ppermute | solution.py:287
  39.3 8.7 %collective-permute-start.10 = (f32[144,128]{1,0:T(8,128)S(1)}, f32[144,128]{1,0:T(8,128)S(1)}, u32[]{:S(2)}, u32[]{:S(2)}) collective-permute-start(f32[144,128]{1,0:T(8,128)S(1)} %get-tuple-element.15), channel_id=1, source_target_pairs={{0,12},{1,13},{2,14},{3,15},{4,8},{5,9},{6,10},{7,11},{8,4},{9,5},... | collective-permute-start | bytes 221192 | tf_op jit(solution)/shard_map/ppermute | solution.py:287
  39.5 8.2 %collective-permute-start.9 = (f32[144,128]{1,0:T(8,128)S(1)}, f32[144,128]{1,0:T(8,128)S(1)}, u32[]{:S(2)}, u32[]{:S(2)}) collective-permute-start(f32[144,128]{1,0:T(8,128)S(1)} %get-tuple-element.15), channel_id=1, source_target_pairs={{0,8},{1,9},{2,10},{3,11},{4,12},{5,13},{6,14},{7,15},{8,0},{9,1},... | collective-permute-start | bytes 221192 | tf_op jit(solution)/shard_map/ppermute | solution.py:287
  47.7 7.0 %collective-permute-start.14 = (f32[144,128]{1,0:T(8,128)S(1)}, f32[144,128]{1,0:T(8,128)S(1)}, u32[]{:S(2)}, u32[]{:S(2)}) collective-permute-start(f32[144,128]{1,0:T(8,128)S(1)} %get-tuple-element.15), channel_id=1, source_target_pairs={{0,28},{1,29},{2,30},{3,31},{4,24},{5,25},{6,26},{7,27},{8,20},{9,... | collective-permute-start | bytes 221192 | tf_op jit(solution)/shard_map/ppermute | solution.py:287
  54.7 2.1 %collective-permute-start.15 = (f32[1152,128]{1,0:T(8,128)S(1)}, f32[1152,128]{1,0:T(8,128)S(1)}, u32[]{:S(2)}, u32[]{:S(2)}) collective-permute-start(f32[1152,128]{1,0:T(8,128)S(1)} %bitcast.74), channel_id=1, source_target_pairs={{0,1},{1,0},{2,3},{3,2},{4,5},{5,4},{6,7},{7,6},{8,9},{9,8},{10,11... | collective-permute-start | bytes 1769480 | tf_op jit(solution)/shard_map/ppermute | solution.py:287
  54.9 2.0 %copy-start.6 = (f32[2,256,256]{2,1,0:T(8,128)S(1)}, f32[2,256,256]{2,1,0:T(8,128)}, u32[]{:S(2)}) copy-start(f32[2,256,256]{2,1,0:T(8,128)} %coupling.2) | copy-start | bytes 1572868
  56.8 30.8 %copy-start.3 = (f32[2048,256]{1,0:T(8,128)S(1)}, f32[2048,256]{1,0:T(8,128)}, u32[]{:S(2)}) copy-start(f32[2048,256]{1,0:T(8,128)} %q_one.5) | copy-start | bytes 6291460
  56.9 30.7 %copy-start.1 = (f32[2048,256]{1,0:T(8,128)S(1)}, f32[2048,256]{1,0:T(8,128)}, u32[]{:S(2)}) copy-start(f32[2048,256]{1,0:T(8,128)} %q_two.5) | copy-start | bytes 6291460
  79.7 7.7 %collective-permute-start.16 = (f32[448,128]{1,0:T(8,128)S(1)}, f32[448,128]{1,0:T(8,128)S(1)}, u32[]{:S(2)}, u32[]{:S(2)}) collective-permute-start(f32[448,128]{1,0:T(8,128)S(1)} %dynamic-slice_bitcast_fusion.1), channel_id=1, source_target_pairs={{0,2},{1,3},{2,0},{3,1},{4,6},{5,7},{6,4},{7,5},{8,10},{9,11},{10,... | collective-permute-start | bytes 688136 | tf_op jit(solution)/shard_map/ppermute | solution.py:287
  87.5 2.9 %collective-permute-start.17 = (f32[448,128]{1,0:T(8,128)S(1)}, f32[448,128]{1,0:T(8,128)S(1)}, u32[]{:S(2)}, u32[]{:S(2)}) collective-permute-start(f32[448,128]{1,0:T(8,128)S(1)} %get-tuple-element.13), channel_id=1, source_target_pairs={{0,1},{1,0},{2,3},{3,2},{4,5},{5,4},{6,7},{7,6},{8,9},{9,8},{10,11... | collective-permute-start | bytes 688136 | tf_op jit(solution)/shard_map/ppermute | solution.py:287
  87.6 2.8 %copy-start.7 = (f32[256,256]{1,0:T(8,128)S(1)}, f32[256,256]{1,0:T(8,128)}, u32[]{:S(2)}) copy-start(f32[256,256]{1,0:T(8,128)} %coupling.3) | copy-start | bytes 786436
  87.6 25.5 %copy-start.5 = (f32[2048,256]{1,0:T(8,128)S(1)}, f32[2048,256]{1,0:T(8,128)}, u32[]{:S(2)}) copy-start(f32[2048,256]{1,0:T(8,128)} %sources.3) | copy-start | bytes 6291460
